TPU v7x, 256 devices: a whole 4x4x8 slice. The times are simulated.
256 devices in a mesh: lon: 32 (over z_lo, y, core), mem: 8 (over z_hi, x).
Axes of the slice: x: 4, y: 4, z: 8 (z_hi: 2, z_lo: 4; z = z_hi * 4 + z_lo), core: 2. Of those that a mesh axis runs over, the one named last changes fastest.
Arguments:
- anomalies: bfloat16 [64, 512, 8192], P('mem', None, 'lon'), may hold values from -6 to 6
- increment: bfloat16 [512, 8192], P(None, 'lon'), may hold values from -6 to 6
- spectral_taper: float32 [8192], replicated, may hold values from 0.05 to 1
Outputs:
- covariance_product: float32 [512, 8192], P(None, 'lon')
All inputs are finite; a program needn't handle non-finite values.
Results may differ from a plain program's by a relative error of at most 0.0011.
Values may be sent and summed in bfloat16 or wider, within the bound.
A program may use at most 128 MiB of HBM per device.

v0:
```python
import math

import jax
import jax.numpy as jnp
from jax import lax
from jax.sharding import PartitionSpec as P

NLON = 8192
FA = 64
FB = 128


def angle_table(row_count, column_count, period):
    left = jnp.arange(row_count, dtype=jnp.int32)[:, None]
    right = jnp.arange(column_count, dtype=jnp.int32)[None, :]
    phase = (left * right % period).astype(jnp.float32) * (2.0 * math.pi / period)
    return (jnp.cos(phase), jnp.sin(phase))


def contract(form, first, second):
    return jnp.einsum(form, first, second, precision=lax.Precision.HIGH)


def localize_rows(fields, spectral_taper):
    cosine_a, sine_a = angle_table(FA, FA, FA)
    cosine_b, sine_b = angle_table(FB, FB, FB)
    twist_cos, twist_sin = angle_table(FA, FB, NLON)
    grid = fields.reshape(-1, FA, FB)
    first_real = contract("kn,rnm->rkm", cosine_a, grid)
    first_imag = -contract("kn,rnm->rkm", sine_a, grid)
    turned_real = first_real * twist_cos + first_imag * twist_sin
    turned_imag = first_imag * twist_cos - first_real * twist_sin
    weights = spectral_taper.reshape(FB, FA).T
    spectrum_real = (
        contract("rkm,mj->rkj", turned_real, cosine_b)
        + contract("rkm,mj->rkj", turned_imag, sine_b)
    ) * weights
    spectrum_imag = (
        contract("rkm,mj->rkj", turned_imag, cosine_b)
        - contract("rkm,mj->rkj", turned_real, sine_b)
    ) * weights
    back_real = contract("rkj,jm->rkm", spectrum_real, cosine_b) - contract(
        "rkj,jm->rkm", spectrum_imag, sine_b
    )
    back_imag = contract("rkj,jm->rkm", spectrum_imag, cosine_b) + contract(
        "rkj,jm->rkm", spectrum_real, sine_b
    )
    reverted_real = back_real * twist_cos - back_imag * twist_sin
    reverted_imag = back_imag * twist_cos + back_real * twist_sin
    result = contract("nk,rkm->rnm", cosine_a, reverted_real) - contract(
        "nk,rkm->rnm", sine_a, reverted_imag
    )
    return result.reshape(-1, NLON) / NLON


def per_device(anomalies, increment, spectral_taper):
    member_total = lax.axis_size("mem") * anomalies.shape[0]
    products = (anomalies.astype(jnp.float32) * increment.astype(jnp.float32)[None]).astype(
        jnp.bfloat16
    )
    circles = lax.all_to_all(products, "lon", split_axis=1, concat_axis=2, tiled=True)
    rows = localize_rows(circles.reshape(-1, NLON).astype(jnp.float32), spectral_taper)
    shaped = rows.astype(jnp.bfloat16).reshape(circles.shape)
    filtered = lax.all_to_all(shaped, "lon", split_axis=2, concat_axis=1, tiled=True)
    partial_sum = jnp.sum(anomalies.astype(jnp.float32) * filtered.astype(jnp.float32), axis=0)
    summed = lax.psum(partial_sum, "mem")
    return summed / (member_total - 1)


def solution(mesh):
    in_specs = (P("mem", None, "lon"), P(None, "lon"), P())
    out_specs = P(None, "lon")
    return jax.shard_map(
        per_device, mesh=mesh, in_specs=in_specs, out_specs=out_specs, check_vma=False
    )
```

profile of v0, /device:TPU:8, one launch (start us, length us, event | category | flops | bytes accessed | tf_op | source)
XLA Modules:
  0.0 372.0 jit_solution(3405150805777882802)
XLA Ops:
  6.5 1.0 convert_element_type.84
  7.5 4.3 %fusion = bf16[8,512,256]{2,0,1:T(8,128)(2,1)} fusion(f32[512,256]{1,0:T(8,128)S(1)} %convert_element_type.84, bf16[8,512,256]{2,1,0:T(8,128)(2,1)} %param.3), kind=kLoop, calls=%fused_computation.2 | loop fusion | flops 3145728 | bytes 4718592 | tf_op jit(solution)/shard_map/convert_element_type | solution.py:58
  11.8 9.1 %all-to-all-start = ((bf16[8,512,256]{2,0,1:T(8,128)(2,1)}), bf16[8,512,256]{2,0,1:T(8,128)(2,1)S(1)}, u32[]{:S(2)}, u32[]{:S(2)}) async-start(bf16[8,512,256]{2,0,1:T(8,128)(2,1)} %fusion), calls=%async_computation | async-start | bytes 4194304 | tf_op jit(solution)/shard_map/all_to_all | solution.py:61
  21.0 0.0 all-reduce.2.cloned.1.call-start
  21.0 0.1 reshape.58
  21.1 0.1 copy.29
  21.2 0.2 fusion.87
  21.4 48.0 %all-to-all-done = bf16[8,512,256]{2,0,1:T(8,128)(2,1)S(1)} async-done(((bf16[8,512,256]{2,0,1:T(8,128)(2,1)}), bf16[8,512,256]{2,0,1:T(8,128)(2,1)S(1)}, u32[]{:S(2)}, u32[]{:S(2)}) %all-to-all-start) | async-done | bytes 2097184 | tf_op jit(solution)/shard_map/all_to_all | solution.py:61
  69.4 2.5 copy.71
  71.9 2.9 reshape.57
  74.8 1.4 fusion.66
  76.2 2.3 fusion.2
  78.4 5.2 %fusion.20 = f32[128,64,128]{2,0,1:T(8,128)S(1)} fusion(f32[128,64,128]{2,1,0:T(8,128)S(1)} %get-tuple-element.6), kind=kOutput, calls=%fused_computation.29 | convolution fusion | flops 805535744 | bytes 8388608 | tf_op jit(solution)/shard_map/rkm,mj->rkj/dot_general | solution.py:21
  83.7 5.6 %fusion.22 = f32[128,64,128]{2,0,1:T(8,128)S(1)} fusion(f32[128,64,128]{2,1,0:T(8,128)S(1)} %get-tuple-element.6), kind=kOutput, calls=%fused_computation.31 | convolution fusion | flops 805535744 | bytes 8388608 | tf_op jit(solution)/shard_map/rkm,mj->rkj/dot_general | solution.py:21
  89.3 5.3 %subtract_multiply_fusion = f32[128,64,128]{2,0,1:T(8,128)S(1)} fusion(f32[128,64,128]{2,0,1:T(8,128)S(1)} %fusion.20, f32[128,64,128]{2,1,0:T(8,128)S(1)} %get-tuple-element.5, f32[64,128]{1,0:T(8,128)S(1)} %copy.29), kind=kOutput, calls=%fused_computation.19 | convolution fusion | flops 807632896 | bytes 12615680 | tf_op jit(solution)/shard_map/rkm,mj->rkj/dot_general | solution.py:21
  94.5 4.9 %fusion.12 = f32[128,64,128]{2,1,0:T(8,128)S(1)} fusion(f32[128,64,128]{2,0,1:T(8,128)S(1)} %subtract_multiply_fusion), kind=kOutput, calls=%fused_computation.21 | convolution fusion | flops 805535744 | bytes 8388608 | tf_op jit(solution)/shard_map/rkj,jm->rkm/dot_general | solution.py:21
  99.4 4.7 %fusion.14 = f32[128,64,128]{2,1,0:T(8,128)S(1)} fusion(f32[128,64,128]{2,0,1:T(8,128)S(1)} %subtract_multiply_fusion), kind=kOutput, calls=%fused_computation.23 | convolution fusion | flops 805535744 | bytes 8388608 | tf_op jit(solution)/shard_map/rkj,jm->rkm/dot_general | solution.py:21
  104.1 5.3 %add_multiply_fusion = f32[128,64,128]{2,0,1:T(8,128)S(1)} fusion(f32[128,64,128]{2,0,1:T(8,128)S(1)} %fusion.22, f32[128,64,128]{2,1,0:T(8,128)S(1)} %get-tuple-element.5, f32[64,128]{1,0:T(8,128)S(1)} %copy.29), kind=kOutput, calls=%fused_computation.20 | convolution fusion | flops 807632896 | bytes 12615680 | tf_op jit(solution)/shard_map/rkm,mj->rkj/dot_general | solution.py:21
  109.4 5.0 %fusion.31 = f32[128,64,128]{2,1,0:T(8,128)S(1)} fusion(f32[128,64,128]{2,1,0:T(8,128)S(1)} %fusion.12, f32[128,64,128]{2,0,1:T(8,128)S(1)} %add_multiply_fusion), kind=kOutput, calls=%fused_computation.38 | convolution fusion | flops 806584320 | bytes 12582912 | tf_op jit(solution)/shard_map/rkj,jm->rkm/dot_general | solution.py:21
  114.4 4.8 %fusion.28 = f32[128,64,128]{2,1,0:T(8,128)S(1)} fusion(f32[128,64,128]{2,1,0:T(8,128)S(1)} %fusion.14, f32[128,64,128]{2,0,1:T(8,128)S(1)} %add_multiply_fusion), kind=kOutput, calls=%fused_computation.37 | convolution fusion | flops 806584320 | bytes 12582912 | tf_op jit(solution)/shard_map/rkj,jm->rkm/dot_general | solution.py:21
  119.2 2.3 fusion.4
  121.5 3.0 fusion.38
  124.5 2.3 convert_element_type.91
  126.7 14.5 %copy.36 = bf16[8,16,8192]{1,0,2:T(8,128)(2,1)} copy(bf16[8,16,8192]{2,1,0:T(8,128)(2,1)} %convert_element_type.91) | data formatting | bytes 4194304 | tf_op jit(solution)/shard_map/convert_element_type | solution.py:63
  141.3 19.7 %reshape.65 = bf16[32,2,16384]{2,1,0:T(2,128)(2,1)S(1)} reshape(bf16[8192,8,16]{2,1,0:T(8,128)(2,1)} %bitcast.64) | data formatting | bytes 4194304
  161.0 54.4 %all_to_all.24 = bf16[32,2,16384]{2,1,0:T(2,128)(2,1)} all-to-all(bf16[32,2,16384]{2,1,0:T(2,128)(2,1)S(1)} %reshape.65), channel_id=1, replica_groups=mesh['lon'=32,'mem'=8] {'lon'}, dimensions={0} | all-to-all | bytes 4194304 | tf_op jit(solution)/shard_map/all_to_all | solution.py:64
  215.4 16.5 %reshape.66 = bf16[8192,8,16]{2,1,0:T(8,128)(2,1)} reshape(bf16[32,2,16384]{2,1,0:T(2,128)(2,1)} %all_to_all.24) | data formatting | bytes 4194304
  231.9 16.9 %copy.37 = f32[8,16,32,256]{3,0,1,2:T(8,128)} copy(bf16[8,16,32,256]{1,0,3,2:T(8,128)(2,1)} %bitcast.63) | data formatting | bytes 6291456 | tf_op jit(solution)/shard_map/convert_element_type | solution.py:65
  248.8 5.2 %fusion.1 = f32[512,256]{1,0:T(8,128)} fusion(f32[8,16,32,256]{3,0,1,2:T(8,128)} %copy.37, bf16[8,512,256]{2,1,0:T(8,128)(2,1)S(1)} %copy-done), kind=kLoop, calls=%fused_computation.3 | loop fusion | flops 3014656 | bytes 6815744 | tf_op jit(solution)/shard_map/reduce_sum | solution.py:65
  254.0 0.0 all-reduce.2.cloned.1.call-update
  254.0 108.9 %all-reduce.2.cloned.1.call-done = f32[512,256]{1,0:T(8,128)} async-done(((f32[512,256]{1,0:T(8,128)}), f32[512,256]{1,0:T(8,128)}) %all-reduce.2.cloned.1.call-update) | async-done | bytes 524304 | tf_op jit(solution)/shard_map/psum | solution.py:66
  362.9 1.9 broadcast_multiply_fusion
  (4 shorter events, 0.0 us)
Async XLA Ops:
  7.5 13.5 %copy-start.1 = (f32[8192]{0:T(1024)S(1)}, f32[8192]{0:T(1024)}, u32[]{:S(2)}) copy-start(f32[8192]{0:T(1024)} %param.5) | copy-start | bytes 98308
  11.8 57.6 %all-to-all-start = ((bf16[8,512,256]{2,0,1:T(8,128)(2,1)}), bf16[8,512,256]{2,0,1:T(8,128)(2,1)S(1)}, u32[]{:S(2)}, u32[]{:S(2)}) async-start(bf16[8,512,256]{2,0,1:T(8,128)(2,1)} %fusion), calls=%async_computation | async-start | bytes 4194304 | tf_op jit(solution)/shard_map/all_to_all | solution.py:61
  21.0 341.9 %all-reduce.2.cloned.1.call-start = ((), (), s32[]{:S(2)}) async-start(), calls=%async_computation.2 | async-start | bytes 1048576 | tf_op jit(solution)/shard_map/psum | solution.py:66
  231.9 16.9 %copy-start = (bf16[8,512,256]{2,1,0:T(8,128)(2,1)S(1)}, bf16[8,512,256]{2,1,0:T(8,128)(2,1)}, u32[]{:S(2)}) copy-start(bf16[8,512,256]{2,1,0:T(8,128)(2,1)} %param.3) | copy-start | bytes 6291460
Sparse Core Ops, SparseCore 0:
  254.1 108.6 all-reduce.1
where the time goes:
time: 377 us; the launch traced here: 372 us
  waiting for transfers between devices  157 us (42%)
  local copies, waits for them, and re-layouts  75.4 us (20%)
  blocking collectives  54.4 us (14%)
  matrix products  49.6 us (13%)
  between operations  14 us (4%)
  other arithmetic  12.6 us (3%)
  starting transfers between devices  9.18 us (2%)
    psum x1, waiting for transfers between devices, per_device(): summed = lax.psum(partial_sum, 'mem')  109 us
    all_to_all x1, blocking collectives, per_device(): lax.all_to_all(shaped, 'lon', split_axis=2, concat_axis=1, tiled=True)  54.4 us
    dot_general x12, matrix products, contract(): return jnp.einsum(form, first, second, precision=lax.Precision.HIGH)  49.6 us
    all_to_all x1, waiting for transfers between devices, per_device(): lax.all_to_all(products, 'lon', split_axis=1, concat_axis=2, tiled=True)  48 us
    unnamed x6, local copies, waits for them, and re-layouts  36.2 us
    convert_element_type x1, local copies, waits for them, and re-layouts, per_device(): filtered.astype(jnp.float32)  16.9 us
    convert_element_type x2, local copies, waits for them, and re-layouts, per_device(): shaped = rows.astype(jnp.bfloat16).reshape(circles.shape)  16.8 us
    all_to_all x1, starting transfers between devices, per_device(): lax.all_to_all(products, 'lon', split_axis=1, concat_axis=2, tiled=True)  9.14 us
  transfers between devices with their start and end apart: 2, of which 2 were waited for; matrix products, arithmetic and copies ran while one was open for 0% of the time, Pallas kernels for 0%

commit v1 on v0

v1 whole, which is shorter than its diff:
```python
import functools
import math

import jax
import jax.numpy as jnp
import numpy as np
from jax import lax
from jax.experimental import pallas as pl
from jax.experimental.pallas import tpu as pltpu
from jax.sharding import PartitionSpec as P

MESH = pl.DeviceIdType.MESH
NLON = 8192
BLOCKS = 64
WIDE = 128
HALF = BLOCKS // 2
LONS = 32
XS = 4
LATS = 16
CHUNKS = 2
PER = LATS // CHUNKS
MEMBERS = 8
ROWS = PER * MEMBERS
PAIRS = MEMBERS // 2
F32 = jnp.float32
BF16 = jnp.bfloat16


def tables():
    s = np.arange(WIDE)[:, None]
    r = np.arange(BLOCKS)[None, :]
    first = 2 * math.pi * (s * r % BLOCKS) / BLOCKS
    first = np.concatenate([np.cos(first), np.sin(first)], 0)
    c = np.arange(WIDE)[None, :]
    twist = 2 * math.pi * (s * c % NLON) / NLON
    twist = np.stack([np.cos(twist), np.sin(twist)])
    d = np.arange(BLOCKS)[:, None]
    back = 2 * math.pi * (d * c % BLOCKS) / BLOCKS
    back = np.stack([np.cos(back), np.sin(back)]) / (NLON * BLOCKS)
    f = np.arange(40)[:, None]
    d = np.arange(BLOCKS)[None, :]
    here = 2 * math.pi * (f * d % BLOCKS) / BLOCKS
    there = 2 * math.pi * (f * (d + 1) % BLOCKS) / BLOCKS
    again = np.stack([np.cos(here), -np.sin(here), np.cos(there), -np.sin(there)])
    return [np.asarray(t, np.float32) for t in (first, twist, back, again)]


def dft4(x):
    (ar, ai), (br, bi), (cr, ci), (dr, di) = x
    er, ei, fr, fi = ar + cr, ai + ci, ar - cr, ai - ci
    gr, gi, hr, hi = br + dr, bi + di, br - dr, bi - di
    return [(er + gr, ei + gi), (fr + hi, fi - hr), (er - gr, ei - gi), (fr - hi, fi + hr)]


def dft8(x):
    even, odd = dft4(x[0::2]), dft4(x[1::2])
    root = math.sqrt(0.5)
    (ar, ai), (br, bi), (cr, ci), (dr, di) = odd
    turned = [
        (ar, ai),
        ((br + bi) * root, (bi - br) * root),
        (ci, -cr),
        ((di - dr) * root, (dr + di) * -root),
    ]
    low = [(e[0] + t[0], e[1] + t[1]) for e, t in zip(even, turned)]
    high = [(e[0] - t[0], e[1] - t[1]) for e, t in zip(even, turned)]
    return low + high


def swap(x):
    return [(i, r) for r, i in x]


def turn(x, power):
    power = power % BLOCKS
    if power == 0:
        return x
    c = math.cos(2 * math.pi * power / BLOCKS)
    s = -math.sin(2 * math.pi * power / BLOCKS)
    return (x[0] * c - x[1] * s, x[0] * s + x[1] * c)


def high(a, b, dims=((1,), (0,))):
    return lax.dot_general(
        a, b, (dims, ((), ())), precision=lax.Precision.HIGHEST, preferred_element_type=F32
    )


def kernel(
    a_hbm, inc_hbm, taper, first, twist, back, again, out,
    a_in, inc_in, snd, rcv, incb, incf, lines, weights, spec, mid, pout,
    rs_snd, rs_rcv, qb, fr, fin,
    load_sem, inc_send, inc_recv, incx_send, incx_recv, main_send, main_recv,
    rs_send, rs_recv, ret_send, ret_recv, fin_send, fin_recv,
):
    lon, mem = lax.axis_index("lon"), lax.axis_index("mem")
    z, y, k = lon // 8, (lon // 2) % 4, lon % 2
    zhi, x = mem // XS, mem % XS

    load_a = pltpu.make_async_copy(a_hbm, a_in, load_sem.at[0])
    load_i = pltpu.make_async_copy(inc_hbm, inc_in, load_sem.at[1])
    load_a.start()
    load_i.start()

    def peer(s):
        return ((z + s // 8) % 4) * 8 + ((y + (s // 2) % 4) % 4) * 2 + (k + s % 2) % 2

    barrier = pltpu.get_barrier_semaphore()

    @pl.loop(1, LONS)
    def _(s):
        pl.semaphore_signal(
            barrier, inc=1, device_id={"lon": peer(s), "mem": mem}, device_id_type=MESH
        )

    @pl.loop(0, LONS)
    def _(s):
        there = ((zhi + 1) % 2) * XS + x
        pl.semaphore_signal(
            barrier, inc=1, device_id={"lon": peer(s), "mem": there}, device_id_type=MESH
        )

    @pl.loop(1, XS)
    def _(s):
        there = zhi * XS + (x + s) % XS
        pl.semaphore_signal(
            barrier, inc=1, device_id={"lon": lon, "mem": there}, device_id_type=MESH
        )

    load_a.wait()

    @pl.loop(0, LONS)
    def _(t):
        for pair in range(PAIRS):
            one = a_in[2 * pair, pl.ds(t * LATS, LATS), :].astype(F32)
            two = a_in[2 * pair + 1, pl.ds(t * LATS, LATS), :].astype(F32)
            for c in range(CHUNKS):
                both = jnp.concatenate([one[c * PER : (c + 1) * PER], two[c * PER : (c + 1) * PER]])
                snd[c, t, pl.ds(pair * 16, 16), :] = both.astype(BF16)

    load_i.wait()
    pl.semaphore_wait(barrier, 2 * LONS - 1 + XS - 1)

    @pl.when(lon % XS == x)
    def _():
        @pl.loop(1, LONS)
        def _(s):
            there = peer(s)
            pltpu.make_async_remote_copy(
                src_ref=inc_in.at[pl.ds(there * LATS, LATS)], dst_ref=incb.at[x, lon // XS],
                send_sem=inc_send, recv_sem=inc_recv,
                device_id={"lon": there, "mem": mem}, device_id_type=MESH,
            ).start()

        pltpu.make_async_copy(
            inc_in.at[pl.ds(lon * LATS, LATS)], incb.at[x, lon // XS], inc_recv
        ).start()

    for c in range(CHUNKS):
        @pl.loop(1, LONS)
        def _(s):
            there = peer(s)
            pltpu.make_async_remote_copy(
                src_ref=snd.at[c, there], dst_ref=rcv.at[c, lon],
                send_sem=main_send.at[c], recv_sem=main_recv.at[c],
                device_id={"lon": there, "mem": mem}, device_id_type=MESH,
            ).start()

        pltpu.make_async_copy(snd.at[c, lon], rcv.at[c, lon], main_recv.at[c]).start()

    u = high(first[...], taper[...])
    ur, ui = u[:WIDE], u[WIDE:]
    vr = ur * twist[0] - ui * twist[1]
    vi = ur * twist[1] + ui * twist[0]
    line = high(back[0], vr, ((1,), (1,))) - high(back[1], vi, ((1,), (1,)))
    lines[0, :, :WIDE] = high(again[0], line)
    lines[1, :, :WIDE] = high(again[1], line)
    lines[0, :, WIDE:] = high(again[2], line)
    lines[1, :, WIDE:] = high(again[3], line)

    @pl.loop(0, HALF + 1)
    def _(f):
        def toeplitz(part):
            row = jnp.broadcast_to(lines[part, pl.ds(f, 1), :], (WIDE, 2 * WIDE))
            return pltpu.roll(row, 0, 1, stride=1, stride_axis=0)[:, :WIDE]

        real, imag = toeplitz(0), toeplitz(1)
        weights[f, :WIDE, :WIDE] = real.astype(BF16)
        weights[f, WIDE:, WIDE:] = real.astype(BF16)
        weights[f, :WIDE, WIDE:] = imag.astype(BF16)
        weights[f, WIDE:, :WIDE] = (-imag).astype(BF16)

    pltpu.make_async_copy(incb.at[x], incb.at[x], inc_recv).wait()

    @pl.loop(1, XS)
    def _(s):
        there = zhi * XS + (x + s) % XS
        pltpu.make_async_remote_copy(
            src_ref=incb.at[x], dst_ref=incb.at[x], send_sem=incx_send, recv_sem=incx_recv,
            device_id={"lon": lon, "mem": there}, device_id_type=MESH,
        ).start()

    three = pl.ds(0, XS - 1)
    pltpu.make_async_copy(incb.at[three], incb.at[three], incx_recv).wait()

    @pl.loop(0, LONS)
    def _(i):
        incf[i] = incb[i % XS, i // XS].astype(F32)

    def tile(c, q, n):
        return rcv[c, n // 2, pl.ds(q * 16, 16), (n % 2) * WIDE : (n % 2 + 1) * WIDE].astype(F32)

    for c in range(CHUNKS):
        pltpu.make_async_copy(rcv.at[c], rcv.at[c], main_recv.at[c]).wait()

        @pl.loop(0, PAIRS)
        def _(q):
            for n2 in range(8):
                points = []
                for n1 in range(8):
                    n = 8 * n1 + n2
                    both = tile(c, q, n)
                    field = incf[n // 2, c * PER : (c + 1) * PER, (n % 2) * WIDE : (n % 2 + 1) * WIDE]
                    real = (both[:8] * field).astype(BF16).astype(F32)
                    imag = (both[8:] * field).astype(BF16).astype(F32)
                    points.append((real, imag))
                for f1, value in enumerate(dft8(points)):
                    value = turn(value, n2 * f1)
                    mid[f1 * 8 + n2, 0] = value[0]
                    mid[f1 * 8 + n2, 1] = value[1]
            for f1 in range(8):
                points = [(mid[f1 * 8 + n2, 0], mid[f1 * 8 + n2, 1]) for n2 in range(8)]
                for f2, value in enumerate(dft8(points)):
                    f = f1 + 8 * f2
                    spec[f, pl.ds(q * 8, 8), :WIDE] = value[0]
                    spec[f, pl.ds(q * 8, 8), WIDE:] = value[1] if f <= HALF else -value[1]

        for f in range(HALF + 1):
            if f in (0, HALF):
                spec[f] = jnp.dot(spec[f].astype(BF16), weights[f], preferred_element_type=F32)
            else:
                both = jnp.concatenate([spec[f], spec[BLOCKS - f]]).astype(BF16)
                both = jnp.dot(both, weights[f], preferred_element_type=F32)
                spec[f] = both[: ROWS // 2]
                spec[BLOCKS - f] = both[ROWS // 2 :]

        pout[...] = jnp.zeros_like(pout)

        @pl.loop(0, PAIRS)
        def _(q):
            for f1 in range(8):
                points = []
                for f2 in range(8):
                    f = f1 + 8 * f2
                    real = spec[f, pl.ds(q * 8, 8), :WIDE]
                    imag = spec[f, pl.ds(q * 8, 8), WIDE:]
                    points.append((real, imag if f <= HALF else -imag))
                for n2, value in enumerate(swap(dft8(swap(points)))):
                    value = turn(value, -n2 * f1)
                    mid[n2 * 8 + f1, 0] = value[0]
                    mid[n2 * 8 + f1, 1] = value[1]
            for n2 in range(8):
                points = [(mid[n2 * 8 + f1, 0], mid[n2 * 8 + f1, 1]) for f1 in range(8)]
                for n1, value in enumerate(swap(dft8(swap(points)))):
                    n = 8 * n1 + n2
                    both = tile(c, q, n)
                    pout[n] += value[0] * both[:8] + value[1] * both[8:]

        @pl.loop(0, BLOCKS)
        def _(n):
            whole = pout[n]
            for s in range(XS):
                rs_snd[c, s, n] = whole[2 * s : 2 * s + 2]

        @pl.loop(1, XS)
        def _(s):
            there = (x + s) % XS
            pltpu.make_async_remote_copy(
                src_ref=rs_snd.at[c, there], dst_ref=rs_rcv.at[c, s - 1],
                send_sem=rs_send.at[c], recv_sem=rs_recv.at[c],
                device_id={"lon": lon, "mem": zhi * XS + there}, device_id_type=MESH,
            ).start()

        pltpu.make_async_copy(rs_rcv.at[c], rs_rcv.at[c], rs_recv.at[c]).wait()
        qb[c] = rs_snd[c, x] + rs_rcv[c, 0] + rs_rcv[c, 1] + rs_rcv[c, 2]

        for e in range(2):
            @pl.loop(1 - e, LONS)
            def _(s):
                there = peer(s)
                pltpu.make_async_remote_copy(
                    src_ref=qb.at[c, pl.ds(2 * there, 2)], dst_ref=fr.at[c, zhi, lon],
                    send_sem=ret_send.at[c], recv_sem=ret_recv.at[c],
                    device_id={"lon": there, "mem": ((zhi + e) % 2) * XS + x}, device_id_type=MESH,
                ).start()

        pltpu.make_async_copy(
            qb.at[c, pl.ds(2 * lon, 2)], fr.at[c, zhi, lon], ret_recv.at[c]
        ).start()
        pltpu.make_async_copy(fr.at[c], fr.at[c], ret_recv.at[c]).wait()
        fin[c, x] = fr[c, 0] + fr[c, 1]

        @pl.loop(1, XS)
        def _(s):
            there = zhi * XS + (x + s) % XS
            pltpu.make_async_remote_copy(
                src_ref=fin.at[c, x], dst_ref=fin.at[c, x],
                send_sem=fin_send.at[c], recv_sem=fin_recv.at[c],
                device_id={"lon": lon, "mem": there}, device_id_type=MESH,
            ).start()

    for c in range(CHUNKS):
        pltpu.make_async_copy(fin.at[c, three], fin.at[c, three], fin_recv.at[c]).wait()
        for s in range(XS):
            row = c * PER + 2 * s
            out[:, row : row + 2, :WIDE] = fin[c, s, :, 0]
            out[:, row : row + 2, WIDE:] = fin[c, s, :, 1]

    @pl.when(lon % XS == x)
    def _():
        sent = inc_in.at[pl.ds(0, (LONS - 1) * LATS)]
        pltpu.make_async_copy(sent, sent, inc_send).wait()

    pltpu.make_async_copy(incb.at[three], incb.at[three], incx_send).wait()
    for c in range(CHUNKS):
        sent = snd.at[c, pl.ds(0, LONS - 1)]
        pltpu.make_async_copy(sent, sent, main_send.at[c]).wait()
        pltpu.make_async_copy(rs_rcv.at[c], rs_rcv.at[c], rs_send.at[c]).wait()
        sent = fr.at[c, 0]
        pltpu.make_async_copy(sent, sent, ret_send.at[c]).wait()
        sent = fr.at[c, 0, pl.ds(0, LONS - 1)]
        pltpu.make_async_copy(sent, sent, ret_send.at[c]).wait()
        pltpu.make_async_copy(fin.at[c, three], fin.at[c, three], fin_send.at[c]).wait()


def per_device(anomalies, increment, spectral_taper):
    any_space, vmem = pl.BlockSpec(memory_space=pl.ANY), pl.BlockSpec(memory_space=pltpu.VMEM)
    dma = pltpu.SemaphoreType.DMA
    both = (2 * LONS, 2, WIDE)
    total = pl.pallas_call(
        kernel,
        out_shape=jax.ShapeDtypeStruct((LONS, LATS, 2 * WIDE), F32),
        in_specs=[any_space, any_space] + [vmem] * 5,
        out_specs=vmem,
        scratch_shapes=[
            pltpu.VMEM((MEMBERS, LONS * LATS, 2 * WIDE), BF16),
            pltpu.VMEM((LONS * LATS, 2 * WIDE), BF16),
            pltpu.VMEM((CHUNKS, LONS, ROWS, 2 * WIDE), BF16),
            pltpu.VMEM((CHUNKS, LONS, ROWS, 2 * WIDE), BF16),
            pltpu.VMEM((XS, LONS // XS, LATS, 2 * WIDE), BF16),
            pltpu.VMEM((LONS, LATS, 2 * WIDE), F32),
            pltpu.VMEM((2, 40, 2 * WIDE), F32),
            pltpu.VMEM((HALF + 1, 2 * WIDE, 2 * WIDE), BF16),
            pltpu.VMEM((BLOCKS, ROWS // 2, 2 * WIDE), F32),
            pltpu.VMEM((BLOCKS, 2, 8, WIDE), F32),
            pltpu.VMEM((BLOCKS, PER, WIDE), F32),
            pltpu.VMEM((CHUNKS, XS) + both, F32),
            pltpu.VMEM((CHUNKS, XS - 1) + both, F32),
            pltpu.VMEM((CHUNKS,) + both, F32),
            pltpu.VMEM((CHUNKS, 2, LONS, 2, 2, WIDE), F32),
            pltpu.VMEM((CHUNKS, XS, LONS, 2, 2, WIDE), F32),
            dma((2,)), dma, dma, dma, dma, dma((CHUNKS,)), dma((CHUNKS,)),
            dma((CHUNKS,)), dma((CHUNKS,)), dma((CHUNKS,)), dma((CHUNKS,)),
            dma((CHUNKS,)), dma((CHUNKS,)),
        ],
        compiler_params=pltpu.CompilerParams(
            collective_id=0, has_side_effects=True, vmem_limit_bytes=48 << 20
        ),
        name="localize",
    )(anomalies, increment, spectral_taper.reshape(BLOCKS, WIDE), *tables())
    members = lax.axis_size("mem") * MEMBERS
    return total.reshape(LONS * LATS, 2 * WIDE) / (members - 1)


def solution(mesh):
    in_specs = (P("mem", None, "lon"), P(None, "lon"), P())
    return jax.shard_map(
        per_device, mesh=mesh, in_specs=in_specs, out_specs=P(None, "lon"), check_vma=False
    )
```

time: 377 us -> 100 us (0.27)
  the two profiles are of different devices: /device:TPU:8 before, /device:TPU:1 now
where the time goes in v1:
time: 100 us; the launch traced here: 99.8 us
  Pallas kernels  92.1 us (92%)
  local copies, waits for them, and re-layouts  6.83 us (7%)
    pallas_call x1, Pallas kernels, per_device(): pl.pallas_call(kernel, out_shape=jax.ShapeDtypeStruct((LONS, LATS, 2 * WI...  92.1 us
    unnamed x14, local copies, waits for them, and re-layouts  6.83 us

profile of v1, /device:TPU:1, one launch (start us, length us, event | category | flops | bytes accessed | tf_op | source)
XLA Modules:
  0.0 99.8 jit_solution(17976025198989570431)
XLA Ops:
  0.0 0.0 copy-start
  0.0 1.6 %copy-done = bf16[8,512,256]{2,1,0:T(8,128)(2,1)S(1)} copy-done((bf16[8,512,256]{2,1,0:T(8,128)(2,1)S(1)}, bf16[8,512,256]{2,1,0:T(8,128)(2,1)}, u32[]{:S(2)}) %copy-start) | copy-done | bytes 2097176
  1.6 0.0 copy-start.1
  1.6 0.9 copy-done.1
  2.5 0.0 copy-start.2
  2.5 0.9 copy-done.2
  3.4 0.0 copy-start.3
  3.4 0.9 copy-done.3
  4.4 0.0 copy-start.4
  4.4 0.9 copy-done.4
  5.2 0.0 copy-start.5
  5.2 0.8 copy-done.5
  6.1 0.0 copy-start.6
  6.1 0.8 copy-done.6
  6.8 92.1 %localize.1 = f32[32,16,256]{2,1,0:T(8,128)S(1)} custom-call(bf16[8,512,256]{2,1,0:T(8,128)(2,1)S(1)} %copy-done, bf16[512,256]{1,0:T(8,128)(2,1)S(1)} %copy-done.1, f32[64,128]{1,0:T(8,128)S(1)} %bitcast.2, f32[256,64]{1,0:T(8,128)S(1)} %copy-done.3, f32[2,128,128]{2,1,0:T(8,128)S(1)} %copy-done.2, f32[2,64,128]{2,1,0:T(8,128)S(1)} %copy-done.5, ...), custom_call_target="tpu_custom_call" | custom-call | tf_op jit(solution)/shard_map/localize/pallas_call | solution.py:340
  99.0 0.8 broadcast_multiply_fusion
Async XLA Ops:
  0.0 1.6 %copy-start = (bf16[8,512,256]{2,1,0:T(8,128)(2,1)S(1)}, bf16[8,512,256]{2,1,0:T(8,128)(2,1)}, u32[]{:S(2)}) copy-start(bf16[8,512,256]{2,1,0:T(8,128)(2,1)} %a_hbm.1) | copy-start | bytes 6291460
  1.6 0.9 copy-start.1
  2.5 0.9 copy-start.2
  3.4 0.9 copy-start.3
  4.4 0.9 copy-start.4
  5.2 0.8 copy-start.5
  6.1 0.8 copy-start.6

commit v2 on v1

v2 whole, which is shorter than its diff:
```python
import functools
import math

import jax
import jax.numpy as jnp
import numpy as np
from jax import lax
from jax.experimental import pallas as pl
from jax.experimental.pallas import tpu as pltpu
from jax.sharding import PartitionSpec as P

MESH = pl.DeviceIdType.MESH
NLON = 8192
BLOCKS = 64
WIDE = 128
HALF = BLOCKS // 2
LONS = 32
XS = 4
LATS = 16
CHUNKS = 4
AHEAD = 2
MIXED = 2
PER = LATS // CHUNKS
MEMBERS = 8
ROWS = PER * MEMBERS
PAIRS = ROWS // 16
F32 = jnp.float32
BF16 = jnp.bfloat16


def tables():
    s = np.arange(WIDE)[:, None]
    r = np.arange(BLOCKS)[None, :]
    first = 2 * math.pi * (s * r % BLOCKS) / BLOCKS
    first = np.concatenate([np.cos(first), np.sin(first)], 0)
    c = np.arange(WIDE)[None, :]
    twist = 2 * math.pi * (s * c % NLON) / NLON
    twist = np.stack([np.cos(twist), np.sin(twist)])
    d = np.arange(BLOCKS)[:, None]
    back = 2 * math.pi * (d * c % BLOCKS) / BLOCKS
    back = np.stack([np.cos(back), np.sin(back)]) / (NLON * BLOCKS)
    f = np.arange(40)[:, None]
    d = np.arange(BLOCKS)[None, :]
    here = 2 * math.pi * (f * d % BLOCKS) / BLOCKS
    there = 2 * math.pi * (f * (d + 1) % BLOCKS) / BLOCKS
    again = np.stack([np.cos(here), -np.sin(here), np.cos(there), -np.sin(there)])
    return [np.asarray(t, np.float32) for t in (first, twist, back, again)]


def dft4(x):
    (ar, ai), (br, bi), (cr, ci), (dr, di) = x
    er, ei, fr, fi = ar + cr, ai + ci, ar - cr, ai - ci
    gr, gi, hr, hi = br + dr, bi + di, br - dr, bi - di
    return [(er + gr, ei + gi), (fr + hi, fi - hr), (er - gr, ei - gi), (fr - hi, fi + hr)]


def dft8(x):
    even, odd = dft4(x[0::2]), dft4(x[1::2])
    root = math.sqrt(0.5)
    (ar, ai), (br, bi), (cr, ci), (dr, di) = odd
    turned = [
        (ar, ai),
        ((br + bi) * root, (bi - br) * root),
        (ci, -cr),
        ((di - dr) * root, (dr + di) * -root),
    ]
    low = [(e[0] + t[0], e[1] + t[1]) for e, t in zip(even, turned)]
    high = [(e[0] - t[0], e[1] - t[1]) for e, t in zip(even, turned)]
    return low + high


def swap(x):
    return [(i, r) for r, i in x]


def turn(x, power):
    power = power % BLOCKS
    if power == 0:
        return x
    c = math.cos(2 * math.pi * power / BLOCKS)
    s = -math.sin(2 * math.pi * power / BLOCKS)
    return (x[0] * c - x[1] * s, x[0] * s + x[1] * c)


def high(a, b, dims=((1,), (0,))):
    return lax.dot_general(
        a, b, (dims, ((), ())), precision=lax.Precision.HIGHEST, preferred_element_type=F32
    )


def kernel(
    a_hbm, inc_hbm, taper_hbm, first_hbm, twist_hbm, back_hbm, again_hbm, out,
    a_in, inc_in, taper, first, twist, back, again,
    snd, rcv, xsnd, xrcv, incb, incf, lines, weights, spec, mid, pout, rs_snd, rs_rcv, qb, fr, part, fin,
    load_sem, inc_send, inc_recv, incx_send, incx_recv, main_send, main_recv,
    x_send, x_recv, rs_send, rs_recv, ret_send, ret_recv, fin_send, fin_recv, group_sem,
):
    lon, mem = lax.axis_index("lon"), lax.axis_index("mem")
    z, y, k = lon // 8, (lon // 2) % 4, lon % 2
    zhi, x = mem // XS, mem % XS

    def load(source, target, sem):
        copy = pltpu.make_async_copy(source, target, load_sem.at[sem])
        copy.start()
        return copy

    load_a = [load(a_hbm.at[j], a_in.at[j], j) for j in range(MEMBERS)]
    load_i = load(inc_hbm, inc_in, MEMBERS)
    pairs = [(taper_hbm, taper), (first_hbm, first), (twist_hbm, twist), (back_hbm, back), (again_hbm, again)]
    load_t = [load(a, b, MEMBERS + 1 + i) for i, (a, b) in enumerate(pairs)]

    def after(v, d):
        return (v + d) % 4

    zs = [after(z, d) * 8 for d in range(4)]
    ys = [after(y, d) * 2 for d in range(4)]
    ks = [k, 1 - k]
    peers = [zs[s // 8] + ys[s // 2 % 4] + ks[s % 2] for s in range(LONS)]
    xs = [(x + d) % XS for d in range(XS)]
    mems = [zhi * XS + xs[d] for d in range(XS)]
    groups = [mem, (1 - zhi) * XS + x]
    rows16 = [zs[s // 2] + ys[0] + ks[s % 2] for s in range(8)]

    barrier = pltpu.get_barrier_semaphore()

    def greet(there, group):
        pl.semaphore_signal(
            barrier, inc=1, device_id={"lon": there, "mem": group}, device_id_type=MESH
        )

    for s in range(1, LONS):
        greet(peers[s], mem)
    greet(lon, groups[1])
    for d in range(1, XS):
        greet(lon, mems[d])

    def remote(source, target, send, recv, there, group):
        pltpu.make_async_remote_copy(
            src_ref=source, dst_ref=target, send_sem=send, recv_sem=recv,
            device_id={"lon": there, "mem": group}, device_id_type=MESH,
        ).start()

    def local(source, target, sem):
        pltpu.make_async_copy(source, target, sem).start()

    def done(ref, sem):
        pltpu.make_async_copy(ref, ref, sem).wait()

    wanted = lax.broadcasted_iota(jnp.int32, (8, WIDE), 0)
    upper = wanted < PER

    def rearrange(c):
        half, low = c // 2, c % 2 == 0

        @pl.loop(0, LONS)
        def _(t):
            for w in range(2):
                cols = slice(w * WIDE, (w + 1) * WIDE)
                parts = []
                for j in range(MEMBERS):
                    whole = a_in[j, pl.ds(t * LATS, LATS), cols].astype(F32)
                    parts.append(whole[half * 8 : half * 8 + 8])
                for j in range(0, MEMBERS, 4):
                    rows = []
                    for i in (j, j + 2):
                        one, two = parts[i], parts[i + 1]
                        if low:
                            two = pltpu.roll(two, PER, 0)
                        else:
                            one = pltpu.roll(one, PER, 0)
                        rows.append(jnp.where(upper, one, two))
                    snd[c, t, pl.ds(j * PER, 4 * PER), cols] = jnp.concatenate(rows).astype(BF16)

    def gather_x():
        row = lax.broadcasted_iota(jnp.int32, (XS * MEMBERS, MEMBERS * LATS), 0)
        col = lax.broadcasted_iota(jnp.int32, (XS * MEMBERS, MEMBERS * LATS), 1)
        for c in range(MIXED, CHUNKS):
            pick = (col == row % MEMBERS * LATS + c * PER + row // MEMBERS).astype(BF16)

            @pl.loop(0, LONS // 2)
            def _(u):
                picked = []
                for e in range(2):
                    whole = a_in[:, pl.ds((2 * u + e) * LATS, LATS), :]
                    whole = whole.reshape(MEMBERS * LATS, 2 * WIDE)
                    picked.append(jnp.dot(pick, whole, preferred_element_type=F32))
                for s in range(XS):
                    both = [p[s * MEMBERS : (s + 1) * MEMBERS] for p in picked]
                    xsnd[c - MIXED, s, u] = jnp.concatenate(both).astype(BF16)

    def send_x(c):
        m = c - MIXED
        for d in range(1, XS):
            remote(xsnd.at[m, xs[d]], xrcv.at[m, x], x_send.at[m], x_recv.at[m], lon, mems[d])
        local(xsnd.at[m, x], xrcv.at[m, x], x_recv.at[m])

    def rearrange_mixed(c):
        m = c - MIXED
        done(xrcv.at[m], x_recv.at[m])

        @pl.loop(0, LONS // 2)
        def _(u):
            for s in range(0, XS, 2):
                one, two = xrcv[m, s, u].astype(F32), xrcv[m, s + 1, u].astype(F32)
                for e in range(2):
                    both = [v[e * MEMBERS : (e + 1) * MEMBERS] for v in (one, two)]
                    snd[c, 2 * u + e, s * MEMBERS : (s + 2) * MEMBERS] = jnp.concatenate(both).astype(BF16)

    def send_main(c):
        for s in range(1, LONS):
            remote(snd.at[c, peers[s]], rcv.at[c, lon], main_send.at[c], main_recv.at[c], peers[s], mem)
        local(snd.at[c, lon], rcv.at[c, lon], main_recv.at[c])

    for copy in load_a:
        copy.wait()
    rearrange(0)
    load_i.wait()
    pl.semaphore_wait(barrier, LONS + XS - 1)
    pl.semaphore_signal(
        group_sem, inc=1, device_id={"lon": lon, "mem": groups[1]}, device_id_type=MESH
    )

    @pl.when(lon % XS == x)
    def _():
        for s in range(1, LONS):
            block = inc_in.at[pl.ds(peers[s] * LATS, LATS)]
            remote(block, incb.at[x, lon // XS], inc_send, inc_recv, peers[s], mem)
        local(inc_in.at[pl.ds(lon * LATS, LATS)], incb.at[x, lon // XS], inc_recv)

    send_main(0)
    gather_x()
    for c in range(MIXED, CHUNKS):
        send_x(c)
    for c in range(1, MIXED):
        rearrange(c)
        if c < AHEAD:
            send_main(c)
    for c in range(MIXED, AHEAD):
        rearrange_mixed(c)
        send_main(c)

    for copy in load_t:
        copy.wait()

    u = high(first[...], taper[...])
    ur, ui = u[:WIDE], u[WIDE:]
    vr = ur * twist[0] - ui * twist[1]
    vi = ur * twist[1] + ui * twist[0]
    line = high(back[0], vr, ((1,), (1,))) - high(back[1], vi, ((1,), (1,)))
    lines[0, :, :WIDE] = high(again[0], line)
    lines[1, :, :WIDE] = high(again[1], line)
    lines[0, :, WIDE:] = high(again[2], line)
    lines[1, :, WIDE:] = high(again[3], line)

    @pl.loop(0, HALF + 1)
    def _(f):
        def toeplitz(part):
            row = jnp.broadcast_to(lines[part, pl.ds(f, 1), :], (WIDE, 2 * WIDE))
            return pltpu.roll(row, 0, 1, stride=1, stride_axis=0)[:, :WIDE]

        real, imag = toeplitz(0), toeplitz(1)
        weights[f, :WIDE, :WIDE] = real.astype(BF16)
        weights[f, WIDE:, WIDE:] = real.astype(BF16)
        weights[f, :WIDE, WIDE:] = imag.astype(BF16)
        weights[f, WIDE:, :WIDE] = (-imag).astype(BF16)

    done(incb.at[x], inc_recv)
    for d in range(1, XS):
        remote(incb.at[x], incb.at[x], incx_send, incx_recv, lon, mems[d])
    three = pl.ds(0, XS - 1)
    done(incb.at[three], incx_recv)

    @pl.loop(0, LONS)
    def _(i):
        for w in range(2):
            whole = incb[i % XS, i // XS, :, w * WIDE : (w + 1) * WIDE].astype(F32)
            for c in range(CHUNKS):
                part = whole[c // 2 * 8 : c // 2 * 8 + 8]
                turned = pltpu.roll(part, PER, 0)
                one, two = (part, turned) if c % 2 == 0 else (turned, part)
                if c < MIXED:
                    incf[c, 2 * i + w] = jnp.where(upper, one, two)
                else:
                    mine = jnp.where(wanted == c % 2 * PER + x, part, 0.0)
                    mine = jnp.sum(mine, axis=0, keepdims=True)
                    incf[c, 2 * i + w] = jnp.broadcast_to(mine, (8, WIDE))

    def tile(c, q, n):
        return rcv[c, n // 2, pl.ds(q * 16, 16), (n % 2) * WIDE : (n % 2 + 1) * WIDE].astype(F32)

    def convolve(c):
        @pl.loop(0, PAIRS)
        def _(q):
            for n2 in range(8):
                points = []
                for n1 in range(8):
                    n = 8 * n1 + n2
                    both = tile(c, q, n)
                    field = incf[c, n]
                    real = (both[:8] * field).astype(BF16).astype(F32)
                    imag = (both[8:] * field).astype(BF16).astype(F32)
                    points.append((real, imag))
                for f1, value in enumerate(dft8(points)):
                    value = turn(value, n2 * f1)
                    mid[f1 * 8 + n2, 0] = value[0]
                    mid[f1 * 8 + n2, 1] = value[1]
            for f1 in range(8):
                points = [(mid[f1 * 8 + n2, 0], mid[f1 * 8 + n2, 1]) for n2 in range(8)]
                for f2, value in enumerate(dft8(points)):
                    f = f1 + 8 * f2
                    spec[f, pl.ds(q * 8, 8), :WIDE] = value[0]
                    spec[f, pl.ds(q * 8, 8), WIDE:] = value[1] if f <= HALF else -value[1]
            pass

        for f in range(HALF + 1):
            if f in (0, HALF):
                spec[f] = jnp.dot(spec[f].astype(BF16), weights[f], preferred_element_type=F32)
            else:
                both = jnp.concatenate([spec[f], spec[BLOCKS - f]]).astype(BF16)
                both = jnp.dot(both, weights[f], preferred_element_type=F32)
                spec[f] = both[: ROWS // 2]
                spec[BLOCKS - f] = both[ROWS // 2 :]

        pout[...] = jnp.zeros_like(pout)

        @pl.loop(0, PAIRS)
        def _(q):
            for f1 in range(8):
                points = []
                for f2 in range(8):
                    f = f1 + 8 * f2
                    real = spec[f, pl.ds(q * 8, 8), :WIDE]
                    imag = spec[f, pl.ds(q * 8, 8), WIDE:]
                    points.append((real, imag if f <= HALF else -imag))
                for n2, value in enumerate(swap(dft8(swap(points)))):
                    value = turn(value, -n2 * f1)
                    mid[n2 * 8 + f1, 0] = value[0]
                    mid[n2 * 8 + f1, 1] = value[1]
            for n2 in range(8):
                points = [(mid[n2 * 8 + f1, 0], mid[n2 * 8 + f1, 1]) for f1 in range(8)]
                for n1, value in enumerate(swap(dft8(swap(points)))):
                    n = 8 * n1 + n2
                    both = tile(c, q, n)
                    pout[n] += value[0] * both[:8] + value[1] * both[8:]
            pass

        @pl.loop(0, BLOCKS // 2)
        def _(i):
            zk, row = i // 8 * 2 + i % 2, i // 2 % 4
            for w in range(2):
                whole = pout[2 * i + w]
                whole = whole + pltpu.roll(whole, 4, 0)
                if c < MIXED:
                    for s in range(XS):
                        rs_snd[c, s, zk, row, w : w + 1] = whole[s : s + 1]
                else:
                    whole = whole + pltpu.roll(whole, 2, 0)
                    whole = whole + pltpu.roll(whole, 1, 0)
                    qb[c, zk, row, w : w + 1] = whole[:1]

    def send_sums(c):
        for d in range(1, XS):
            remote(rs_snd.at[c, xs[d]], rs_rcv.at[c, d - 1], rs_send.at[c], rs_recv.at[c], lon, mems[d])

    def send_back(c):
        if c < MIXED:
            done(rs_rcv.at[c], rs_recv.at[c])
            qb[c] = rs_snd[c, x] + rs_rcv[c, 0] + rs_rcv[c, 1] + rs_rcv[c, 2]
        for g in (1, 0):
            for s in range(8):
                if g or s:
                    index = zs[s // 2] // 4 + ks[s % 2]
                    remote(
                        qb.at[c, index], fr.at[c, zhi, z * 2 + k], ret_send.at[c], ret_recv.at[c],
                        rows16[s], groups[g],
                    )
        local(qb.at[c, z * 2 + k], fr.at[c, zhi, z * 2 + k], ret_recv.at[c])

    def send_all(c):
        done(fr.at[c], ret_recv.at[c])
        for row in range(4):
            part[c, row] = fr[c, 0, :, row] + fr[c, 1, :, row]
        for d in (2, 1, 3, 0):
            for e in (2, 1, 3, 0):
                if d or e:
                    there = z * 8 + ys[e] + k
                    remote(part.at[c, ys[e] // 2], fin.at[c, x, y], fin_send.at[c], fin_recv.at[c], there, mems[d])
        local(part.at[c, y], fin.at[c, x, y], fin_recv.at[c])

    def assemble(c):
        done(fin.at[c], fin_recv.at[c])

        @pl.loop(0, 4)
        def _(row):
            for s in range(XS):
                for i in range(8):
                    at = c * PER + s
                    out[i // 2 * 8 + row * 2 + i % 2, at : at + 1, :WIDE] = fin[c, s, row, i, 0:1]
                    out[i // 2 * 8 + row * 2 + i % 2, at : at + 1, WIDE:] = fin[c, s, row, i, 1:2]

    for step in range(CHUNKS):
        done(rcv.at[step], main_recv.at[step])
        later = step + AHEAD
        if later < CHUNKS:
            if later >= MIXED:
                rearrange_mixed(later)
            send_main(later)
        convolve(step)
        if step == 0:
            pl.semaphore_wait(group_sem, 1)
        if step < MIXED:
            send_sums(step)
        else:
            send_back(step)
        if 1 <= step <= MIXED:
            send_back(step - 1)
        if step >= 2:
            send_all(step - 2)

    for c in range(CHUNKS - 2, CHUNKS):
        if c == MIXED - 1 == CHUNKS - 1:
            send_back(c)
        send_all(c)
    for c in range(CHUNKS):
        assemble(c)

    @pl.when(lon % XS == x)
    def _():
        done(inc_in.at[pl.ds(0, (LONS - 1) * LATS)], inc_send)

    done(incb.at[three], incx_send)
    for c in range(CHUNKS):
        done(snd.at[c, pl.ds(0, LONS - 1)], main_send.at[c])
        if c >= MIXED:
            done(xsnd.at[c - MIXED, three], x_send.at[c - MIXED])
        if c < MIXED:
            done(rs_rcv.at[c], rs_send.at[c])
        done(fr.at[c, 0], ret_send.at[c])
        done(fr.at[c, 0, pl.ds(0, 7)], ret_send.at[c])
        done(fin.at[c, 0], fin_send.at[c])
        done(fin.at[c, 1], fin_send.at[c])
        done(fin.at[c, 2], fin_send.at[c])
        done(fin.at[c, 0, pl.ds(0, 3)], fin_send.at[c])


def per_device(anomalies, increment, spectral_taper):
    hbm, vmem = pl.BlockSpec(memory_space=pltpu.HBM), pl.BlockSpec(memory_space=pltpu.VMEM)
    constants = tables()
    dma = pltpu.SemaphoreType.DMA
    circle = (8, 4, 2, WIDE)
    mixed = (max(CHUNKS - MIXED, 1), XS, LONS // 2, 2 * MEMBERS, 2 * WIDE)
    total = pl.pallas_call(
        kernel,
        out_shape=jax.ShapeDtypeStruct((LONS, LATS, 2 * WIDE), F32),
        in_specs=[hbm] * 7,
        out_specs=vmem,
        scratch_shapes=[
            pltpu.VMEM((MEMBERS, LONS * LATS, 2 * WIDE), BF16),
            pltpu.VMEM((LONS * LATS, 2 * WIDE), BF16),
            pltpu.VMEM((BLOCKS, WIDE), F32),
        ]
        + [pltpu.VMEM(t.shape, F32) for t in constants]
        + [
            pltpu.VMEM((CHUNKS, LONS, ROWS, 2 * WIDE), BF16),
            pltpu.VMEM((CHUNKS, LONS, ROWS, 2 * WIDE), BF16),
            pltpu.VMEM(mixed, BF16),
            pltpu.VMEM(mixed, BF16),
            pltpu.VMEM((XS, LONS // XS, LATS, 2 * WIDE), BF16),
            pltpu.VMEM((CHUNKS, BLOCKS, 8, WIDE), F32),
            pltpu.VMEM((2, 40, 2 * WIDE), F32),
            pltpu.VMEM((HALF + 1, 2 * WIDE, 2 * WIDE), BF16),
            pltpu.VMEM((BLOCKS, ROWS // 2, 2 * WIDE), F32),
            pltpu.VMEM((BLOCKS, 2, 8, WIDE), F32),
            pltpu.VMEM((BLOCKS, 8, WIDE), F32),
            pltpu.VMEM((CHUNKS, XS) + circle, F32),
            pltpu.VMEM((CHUNKS, XS - 1) + circle, F32),
            pltpu.VMEM((CHUNKS,) + circle, F32),
            pltpu.VMEM((CHUNKS, 2) + circle, F32),
            pltpu.VMEM((CHUNKS, 4, 8, 2, WIDE), F32),
            pltpu.VMEM((CHUNKS, XS, 4, 8, 2, WIDE), F32),
            dma((MEMBERS + 6,)), dma, dma, dma, dma, dma((CHUNKS,)), dma((CHUNKS,)),
            dma((CHUNKS,)), dma((CHUNKS,)), dma((CHUNKS,)), dma((CHUNKS,)), dma((CHUNKS,)), dma((CHUNKS,)),
            dma((CHUNKS,)), dma((CHUNKS,)), pltpu.SemaphoreType.REGULAR,
        ],
        compiler_params=pltpu.CompilerParams(
            collective_id=0, has_side_effects=True, vmem_limit_bytes=62 << 20
        ),
        name="localize",
    )(anomalies, increment, spectral_taper.reshape(BLOCKS, WIDE), *constants)
    members = lax.axis_size("mem") * MEMBERS
    return total.reshape(LONS * LATS, 2 * WIDE) / (members - 1)


def solution(mesh):
    in_specs = (P("mem", None, "lon"), P(None, "lon"), P())
    return jax.shard_map(
        per_device, mesh=mesh, in_specs=in_specs, out_specs=P(None, "lon"), check_vma=False
    )
```

time: 100 us -> 79.5 us (0.80)
  Pallas kernels: 92.1 us -> 77.5 us
  local copies, waits for them, and re-layouts: 6.83 us -> 0 us
  other arithmetic: 0.84 us -> 1.89 us
    pallas_call x1, Pallas kernels: 92.1 us -> 77.5 us  [per_device(): pl.pallas_call(kernel, out_shape=jax.ShapeDtypeStruct((LONS, LATS, 2 * WI...]
    unnamed x14 -> x0, local copies, waits for them, and re-layouts: 6.83 us -> none
    div x1, other arithmetic: 0.84 us -> 1.89 us  [per_device(): return total.reshape(LONS * LATS, 2 * WIDE) / (members - 1)]
where the time goes in v2:
time: 79.5 us; the launch traced here: 79.3 us
  Pallas kernels  77.5 us (97%)
  other arithmetic  1.89 us (2%)
    pallas_call x1, Pallas kernels, per_device(): pl.pallas_call(kernel, out_shape=jax.ShapeDtypeStruct((LONS, LATS, 2 * WI...  77.5 us
    div x1, other arithmetic, per_device(): return total.reshape(LONS * LATS, 2 * WIDE) / (members - 1)  1.89 us

profile of v2, /device:TPU:1, one launch (start us, length us, event | category | flops | bytes accessed | tf_op | source)
XLA Modules:
  0.0 79.3 jit_solution(1815718026897417162)
XLA Ops:
  0.0 77.5 %localize.1 = f32[32,16,256]{2,1,0:T(8,128)} custom-call(bf16[8,512,256]{2,1,0:T(8,128)(2,1)} %a_hbm.1, bf16[512,256]{1,0:T(8,128)(2,1)} %inc_hbm.1, f32[64,128]{1,0:T(8,128)} %bitcast.2, f32[256,64]{1,0:T(8,128)} %constant.11.clone.first_hbm, f32[2,128,128]{2,1,0:T(8,128)} %constant.12.clone.twist_hbm, f32[2,64,128]{2,1,0:T(8,128)} %constant.13.clone.back_hbm, ...), custom_call_target="tpu_custom_call" | custom-call | tf_op jit(solution)/shard_map/localize/pallas_call | solution.py:452
  77.5 1.9 %broadcast_multiply_fusion = f32[32,16,256]{2,1,0:T(8,128)} fusion(f32[32,16,256]{2,1,0:T(8,128)} %localize.1), kind=kLoop, calls=%fused_computation | loop fusion | flops 131072 | bytes 1048576 | tf_op jit(solution)/shard_map/div | solution.py:491

commit v3 on v2

--- a/solution.py
+++ b/solution.py
@@ -18,7 +18,7 @@
 XS = 4
 LATS = 16
 CHUNKS = 4
-AHEAD = 2
+SETS = ((0, 1), (2,), (3,))
 MIXED = 2
 PER = LATS // CHUNKS
 MEMBERS = 8
@@ -91,23 +91,23 @@
 def kernel(
     a_hbm, inc_hbm, taper_hbm, first_hbm, twist_hbm, back_hbm, again_hbm, out,
     a_in, inc_in, taper, first, twist, back, again,
-    snd, rcv, xsnd, xrcv, incb, incf, lines, weights, spec, mid, pout, rs_snd, rs_rcv, qb, fr, part, fin,
+    snd, rcv, xsnd, xrcv, incb, incf, lines, weights, spec, mid, pout, rs_snd, rs_rcv,
     load_sem, inc_send, inc_recv, incx_send, incx_recv, main_send, main_recv,
-    x_send, x_recv, rs_send, rs_recv, ret_send, ret_recv, fin_send, fin_recv, group_sem,
+    x_send, x_recv, rs_send, rs_recv, ret_send, ret_recv, fin_send, fin_recv, group_sem, *sums,
 ):
     lon, mem = lax.axis_index("lon"), lax.axis_index("mem")
     z, y, k = lon // 8, (lon // 2) % 4, lon % 2
     zhi, x = mem // XS, mem % XS
 
+    qb, fr, part, fin = [sums[i * len(SETS) : (i + 1) * len(SETS)] for i in range(4)]
+
     def load(source, target, sem):
         copy = pltpu.make_async_copy(source, target, load_sem.at[sem])
         copy.start()
         return copy
 
-    load_a = [load(a_hbm.at[j], a_in.at[j], j) for j in range(MEMBERS)]
-    load_i = load(inc_hbm, inc_in, MEMBERS)
-    pairs = [(taper_hbm, taper), (first_hbm, first), (twist_hbm, twist), (back_hbm, back), (again_hbm, again)]
-    load_t = [load(a, b, MEMBERS + 1 + i) for i, (a, b) in enumerate(pairs)]
+    group = MEMBERS // 2
+    load_a = [load(a_hbm.at[pl.ds(j * group, group)], a_in.at[pl.ds(j * group, group)], j) for j in range(2)]
 
     def after(v, d):
         return (v + d) % 4
@@ -128,11 +128,15 @@
             barrier, inc=1, device_id={"lon": there, "mem": group}, device_id_type=MESH
         )
 
-    for s in range(1, LONS):
+    greet(lon, groups[1])
+    for s in reversed(range(1, LONS)):
         greet(peers[s], mem)
-    greet(lon, groups[1])
     for d in range(1, XS):
         greet(lon, mems[d])
+
+    load_i = load(inc_hbm, inc_in, 2)
+    pairs = [(taper_hbm, taper), (first_hbm, first), (twist_hbm, twist), (back_hbm, back), (again_hbm, again)]
+    load_t = [load(a, b, 3 + i) for i, (a, b) in enumerate(pairs)]
 
     def remote(source, target, send, recv, there, group):
         pltpu.make_async_remote_copy(
@@ -206,10 +210,12 @@
                     both = [v[e * MEMBERS : (e + 1) * MEMBERS] for v in (one, two)]
                     snd[c, 2 * u + e, s * MEMBERS : (s + 2) * MEMBERS] = jnp.concatenate(both).astype(BF16)
 
-    def send_main(c):
+    def send_main(c, half):
         for s in range(1, LONS):
-            remote(snd.at[c, peers[s]], rcv.at[c, lon], main_send.at[c], main_recv.at[c], peers[s], mem)
-        local(snd.at[c, lon], rcv.at[c, lon], main_recv.at[c])
+            if s % 2 == half:
+                remote(snd.at[c, peers[s]], rcv.at[c, lon], main_send.at[c], main_recv.at[c], peers[s], mem)
+        if half:
+            local(snd.at[c, lon], rcv.at[c, lon], main_recv.at[c])
 
     for copy in load_a:
         copy.wait()
@@ -227,17 +233,17 @@
             remote(block, incb.at[x, lon // XS], inc_send, inc_recv, peers[s], mem)
         local(inc_in.at[pl.ds(lon * LATS, LATS)], incb.at[x, lon // XS], inc_recv)
 
-    send_main(0)
+    send_main(0, 0)
+    send_main(0, 1)
+    for c in range(1, MIXED):
+        rearrange(c)
     gather_x()
+    done(incb.at[x], inc_recv)
+    for d in range(1, XS):
+        remote(incb.at[x], incb.at[x], incx_send, incx_recv, lon, mems[d])
     for c in range(MIXED, CHUNKS):
         send_x(c)
-    for c in range(1, MIXED):
-        rearrange(c)
-        if c < AHEAD:
-            send_main(c)
-    for c in range(MIXED, AHEAD):
-        rearrange_mixed(c)
-        send_main(c)
+    send_main(1, 0)
 
     for copy in load_t:
         copy.wait()
@@ -259,14 +265,9 @@
             return pltpu.roll(row, 0, 1, stride=1, stride_axis=0)[:, :WIDE]
 
         real, imag = toeplitz(0), toeplitz(1)
-        weights[f, :WIDE, :WIDE] = real.astype(BF16)
-        weights[f, WIDE:, WIDE:] = real.astype(BF16)
-        weights[f, :WIDE, WIDE:] = imag.astype(BF16)
-        weights[f, WIDE:, :WIDE] = (-imag).astype(BF16)
-
-    done(incb.at[x], inc_recv)
-    for d in range(1, XS):
-        remote(incb.at[x], incb.at[x], incx_send, incx_recv, lon, mems[d])
+        weights[f, :, :WIDE] = real.astype(BF16)
+        weights[f, :, WIDE:] = imag.astype(BF16)
+
     three = pl.ds(0, XS - 1)
     done(incb.at[three], incx_recv)
 
@@ -313,13 +314,17 @@
             pass
 
         for f in range(HALF + 1):
-            if f in (0, HALF):
-                spec[f] = jnp.dot(spec[f].astype(BF16), weights[f], preferred_element_type=F32)
-            else:
-                both = jnp.concatenate([spec[f], spec[BLOCKS - f]]).astype(BF16)
-                both = jnp.dot(both, weights[f], preferred_element_type=F32)
-                spec[f] = both[: ROWS // 2]
-                spec[BLOCKS - f] = both[ROWS // 2 :]
+            both = [f] if f in (0, HALF) else [f, BLOCKS - f]
+            rows = len(both) * ROWS // 2
+            reals = [spec[g, :, :WIDE] for g in both]
+            imags = [spec[g, :, WIDE:] for g in both]
+            value = jnp.concatenate(reals + imags).astype(BF16)
+            value = jnp.dot(value, weights[f], preferred_element_type=F32)
+            real = value[:rows, :WIDE] - value[rows:, WIDE:]
+            imag = value[:rows, WIDE:] + value[rows:, :WIDE]
+            for i, g in enumerate(both):
+                spec[g, :, :WIDE] = real[i * ROWS // 2 : (i + 1) * ROWS // 2]
+                spec[g, :, WIDE:] = imag[i * ROWS // 2 : (i + 1) * ROWS // 2]
 
         pout[...] = jnp.zeros_like(pout)
 
@@ -356,73 +361,79 @@
                 else:
                     whole = whole + pltpu.roll(whole, 2, 0)
                     whole = whole + pltpu.roll(whole, 1, 0)
-                    qb[c, zk, row, w : w + 1] = whole[:1]
+                    qb[c - MIXED + 1][zk, 0, row, w : w + 1] = whole[:1]
 
     def send_sums(c):
         for d in range(1, XS):
             remote(rs_snd.at[c, xs[d]], rs_rcv.at[c, d - 1], rs_send.at[c], rs_recv.at[c], lon, mems[d])
 
-    def send_back(c):
-        if c < MIXED:
-            done(rs_rcv.at[c], rs_recv.at[c])
-            qb[c] = rs_snd[c, x] + rs_rcv[c, 0] + rs_rcv[c, 1] + rs_rcv[c, 2]
-        for g in (1, 0):
+    def send_back(g):
+        for j, c in enumerate(SETS[g]):
+            if c < MIXED:
+                done(rs_rcv.at[c], rs_recv.at[c])
+                qb[g][:, j] = rs_snd[c, x] + rs_rcv[c, 0] + rs_rcv[c, 1] + rs_rcv[c, 2]
+        mine = z * 2 + k
+        for e in (1, 0):
             for s in range(8):
-                if g or s:
+                if e or s:
                     index = zs[s // 2] // 4 + ks[s % 2]
                     remote(
-                        qb.at[c, index], fr.at[c, zhi, z * 2 + k], ret_send.at[c], ret_recv.at[c],
-                        rows16[s], groups[g],
+                        qb[g].at[index], fr[g].at[zhi, mine], ret_send.at[g], ret_recv.at[g],
+                        rows16[s], groups[e],
                     )
-        local(qb.at[c, z * 2 + k], fr.at[c, zhi, z * 2 + k], ret_recv.at[c])
-
-    def send_all(c):
-        done(fr.at[c], ret_recv.at[c])
-        for row in range(4):
-            part[c, row] = fr[c, 0, :, row] + fr[c, 1, :, row]
+        local(qb[g].at[mine], fr[g].at[zhi, mine], ret_recv.at[g])
+
+    def send_all(g):
+        done(fr[g], ret_recv.at[g])
+        for j in range(len(SETS[g])):
+            for row in range(4):
+                part[g][row, j] = fr[g][0, :, j, row] + fr[g][1, :, j, row]
         for d in (2, 1, 3, 0):
             for e in (2, 1, 3, 0):
                 if d or e:
                     there = z * 8 + ys[e] + k
-                    remote(part.at[c, ys[e] // 2], fin.at[c, x, y], fin_send.at[c], fin_recv.at[c], there, mems[d])
-        local(part.at[c, y], fin.at[c, x, y], fin_recv.at[c])
-
-    def assemble(c):
-        done(fin.at[c], fin_recv.at[c])
+                    remote(
+                        part[g].at[ys[e] // 2], fin[g].at[x, y], fin_send.at[g], fin_recv.at[g],
+                        there, mems[d],
+                    )
+        local(part[g].at[y], fin[g].at[x, y], fin_recv.at[g])
+
+    def assemble(g):
+        done(fin[g], fin_recv.at[g])
 
         @pl.loop(0, 4)
         def _(row):
-            for s in range(XS):
-                for i in range(8):
-                    at = c * PER + s
-                    out[i // 2 * 8 + row * 2 + i % 2, at : at + 1, :WIDE] = fin[c, s, row, i, 0:1]
-                    out[i // 2 * 8 + row * 2 + i % 2, at : at + 1, WIDE:] = fin[c, s, row, i, 1:2]
+            for j, c in enumerate(SETS[g]):
+                for s in range(XS):
+                    for i in range(8):
+                        to, at = i // 2 * 8 + row * 2 + i % 2, c * PER + s
+                        out[to, at : at + 1, :WIDE] = fin[g][s, row, j, i, 0:1]
+                        out[to, at : at + 1, WIDE:] = fin[g][s, row, j, i, 1:2]
 
     for step in range(CHUNKS):
         done(rcv.at[step], main_recv.at[step])
-        later = step + AHEAD
-        if later < CHUNKS:
-            if later >= MIXED:
-                rearrange_mixed(later)
-            send_main(later)
-        convolve(step)
         if step == 0:
             pl.semaphore_wait(group_sem, 1)
+        if step < 2:
+            send_main(step + 1, 1)
+        convolve(step)
         if step < MIXED:
             send_sums(step)
         else:
-            send_back(step)
-        if 1 <= step <= MIXED:
             send_back(step - 1)
-        if step >= 2:
-            send_all(step - 2)
-
-    for c in range(CHUNKS - 2, CHUNKS):
-        if c == MIXED - 1 == CHUNKS - 1:
-            send_back(c)
-        send_all(c)
-    for c in range(CHUNKS):
-        assemble(c)
+        if step < 2:
+            rearrange_mixed(step + 2)
+            send_main(step + 2, 0)
+        if step == 2:
+            send_main(3, 1)
+            send_back(0)
+            send_all(1)
+
+    send_all(0)
+    assemble(1)
+    send_all(2)
+    assemble(0)
+    assemble(2)
 
     @pl.when(lon % XS == x)
     def _():
@@ -435,12 +446,11 @@
             done(xsnd.at[c - MIXED, three], x_send.at[c - MIXED])
         if c < MIXED:
             done(rs_rcv.at[c], rs_send.at[c])
-        done(fr.at[c, 0], ret_send.at[c])
-        done(fr.at[c, 0, pl.ds(0, 7)], ret_send.at[c])
-        done(fin.at[c, 0], fin_send.at[c])
-        done(fin.at[c, 1], fin_send.at[c])
-        done(fin.at[c, 2], fin_send.at[c])
-        done(fin.at[c, 0, pl.ds(0, 3)], fin_send.at[c])
+    for g in range(len(SETS)):
+        done(fr[g].at[0], ret_send.at[g])
+        done(fr[g].at[0, pl.ds(0, 7)], ret_send.at[g])
+        done(fin[g].at[three], fin_send.at[g])
+        done(fin[g].at[0, three], fin_send.at[g])
 
 
 def per_device(anomalies, increment, spectral_taper):
@@ -468,20 +478,20 @@
             pltpu.VMEM((XS, LONS // XS, LATS, 2 * WIDE), BF16),
             pltpu.VMEM((CHUNKS, BLOCKS, 8, WIDE), F32),
             pltpu.VMEM((2, 40, 2 * WIDE), F32),
-            pltpu.VMEM((HALF + 1, 2 * WIDE, 2 * WIDE), BF16),
+            pltpu.VMEM((HALF + 1, WIDE, 2 * WIDE), BF16),
             pltpu.VMEM((BLOCKS, ROWS // 2, 2 * WIDE), F32),
             pltpu.VMEM((BLOCKS, 2, 8, WIDE), F32),
             pltpu.VMEM((BLOCKS, 8, WIDE), F32),
             pltpu.VMEM((CHUNKS, XS) + circle, F32),
             pltpu.VMEM((CHUNKS, XS - 1) + circle, F32),
-            pltpu.VMEM((CHUNKS,) + circle, F32),
-            pltpu.VMEM((CHUNKS, 2) + circle, F32),
-            pltpu.VMEM((CHUNKS, 4, 8, 2, WIDE), F32),
-            pltpu.VMEM((CHUNKS, XS, 4, 8, 2, WIDE), F32),
-            dma((MEMBERS + 6,)), dma, dma, dma, dma, dma((CHUNKS,)), dma((CHUNKS,)),
+            dma((8,)), dma, dma, dma, dma, dma((CHUNKS,)), dma((CHUNKS,)),
             dma((CHUNKS,)), dma((CHUNKS,)), dma((CHUNKS,)), dma((CHUNKS,)), dma((CHUNKS,)), dma((CHUNKS,)),
             dma((CHUNKS,)), dma((CHUNKS,)), pltpu.SemaphoreType.REGULAR,
-        ],
+        ]
+        + [pltpu.VMEM((8, len(g), 4, 2, WIDE), F32) for g in SETS]
+        + [pltpu.VMEM((2, 8, len(g), 4, 2, WIDE), F32) for g in SETS]
+        + [pltpu.VMEM((4, len(g), 8, 2, WIDE), F32) for g in SETS]
+        + [pltpu.VMEM((XS, 4, len(g), 8, 2, WIDE), F32) for g in SETS],
         compiler_params=pltpu.CompilerParams(
             collective_id=0, has_side_effects=True, vmem_limit_bytes=62 << 20
         ),

time: 79.5 us -> 78.5 us (0.987)
  Pallas kernels: 77.5 us -> 76.4 us
    pallas_call x1, Pallas kernels: 77.5 us -> 76.4 us  [per_device(): pl.pallas_call(kernel, out_shape=jax.ShapeDtypeStruct((LONS, LATS, 2 * WI...]
where the time goes in v3:
time: 78.5 us; the launch traced here: 78.3 us
  Pallas kernels  76.4 us (97%)
  other arithmetic  1.89 us (2%)
    pallas_call x1, Pallas kernels, per_device(): pl.pallas_call(kernel, out_shape=jax.ShapeDtypeStruct((LONS, LATS, 2 * WI...  76.4 us
    div x1, other arithmetic, per_device(): return total.reshape(LONS * LATS, 2 * WIDE) / (members - 1)  1.89 us

profile of v3, /device:TPU:1, one launch (start us, length us, event | category | flops | bytes accessed | tf_op | source)
XLA Modules:
  0.0 78.3 jit_solution(532491877390494201)
XLA Ops:
  0.0 76.4 %localize.1 = f32[32,16,256]{2,1,0:T(8,128)} custom-call(bf16[8,512,256]{2,1,0:T(8,128)(2,1)} %a_hbm.1, bf16[512,256]{1,0:T(8,128)(2,1)} %inc_hbm.1, f32[64,128]{1,0:T(8,128)} %bitcast.2, f32[256,64]{1,0:T(8,128)} %constant.11.clone.first_hbm, f32[2,128,128]{2,1,0:T(8,128)} %constant.12.clone.twist_hbm, f32[2,64,128]{2,1,0:T(8,128)} %constant.13.clone.back_hbm, ...), custom_call_target="tpu_custom_call" | custom-call | tf_op jit(solution)/shard_map/localize/pallas_call | solution.py:462
  76.4 1.9 %broadcast_multiply_fusion = f32[32,16,256]{2,1,0:T(8,128)} fusion(f32[32,16,256]{2,1,0:T(8,128)} %localize.1), kind=kLoop, calls=%fused_computation | loop fusion | flops 131072 | bytes 1048576 | tf_op jit(solution)/shard_map/div | solution.py:501

commit v4 on v3

--- a/solution.py
+++ b/solution.py
@@ -211,6 +211,12 @@
                     snd[c, 2 * u + e, s * MEMBERS : (s + 2) * MEMBERS] = jnp.concatenate(both).astype(BF16)
 
     def send_main(c, half):
+        if c == CHUNKS - 1:
+            rows, sem = pl.ds(half * 16, 16), main_recv.at[c + half]
+            for s in range(1, LONS):
+                remote(snd.at[c, peers[s], rows], rcv.at[c, lon, rows], main_send.at[c], sem, peers[s], mem)
+            local(snd.at[c, lon, rows], rcv.at[c, lon, rows], sem)
+            return
         for s in range(1, LONS):
             if s % 2 == half:
                 remote(snd.at[c, peers[s]], rcv.at[c, lon], main_send.at[c], main_recv.at[c], peers[s], mem)
@@ -226,14 +232,18 @@
         group_sem, inc=1, device_id={"lon": lon, "mem": groups[1]}, device_id_type=MESH
     )
 
+    send_main(0, 0)
+    pl.semaphore_wait(group_sem, 1)
+
     @pl.when(lon % XS == x)
     def _():
         for s in range(1, LONS):
             block = inc_in.at[pl.ds(peers[s] * LATS, LATS)]
-            remote(block, incb.at[x, lon // XS], inc_send, inc_recv, peers[s], mem)
+            beyond = (z // 2 + peers[s] // 16) % 2
+            there = (zhi + beyond) % 2 * XS + x
+            remote(block, incb.at[x, lon // XS], inc_send, inc_recv, peers[s], there)
         local(inc_in.at[pl.ds(lon * LATS, LATS)], incb.at[x, lon // XS], inc_recv)
 
-    send_main(0, 0)
     send_main(0, 1)
     for c in range(1, MIXED):
         rearrange(c)
@@ -289,8 +299,9 @@
     def tile(c, q, n):
         return rcv[c, n // 2, pl.ds(q * 16, 16), (n % 2) * WIDE : (n % 2 + 1) * WIDE].astype(F32)
 
-    def convolve(c):
-        @pl.loop(0, PAIRS)
+    def convolve(c, qs):
+        top, count = qs[0] * 8, len(qs) * 8
+        @pl.loop(qs[0], qs[-1] + 1)
         def _(q):
             for n2 in range(8):
                 points = []
@@ -315,20 +326,21 @@
 
         for f in range(HALF + 1):
             both = [f] if f in (0, HALF) else [f, BLOCKS - f]
-            rows = len(both) * ROWS // 2
-            reals = [spec[g, :, :WIDE] for g in both]
-            imags = [spec[g, :, WIDE:] for g in both]
+            rows = len(both) * count
+            reals = [spec[g, top : top + count, :WIDE] for g in both]
+            imags = [spec[g, top : top + count, WIDE:] for g in both]
             value = jnp.concatenate(reals + imags).astype(BF16)
             value = jnp.dot(value, weights[f], preferred_element_type=F32)
             real = value[:rows, :WIDE] - value[rows:, WIDE:]
             imag = value[:rows, WIDE:] + value[rows:, :WIDE]
             for i, g in enumerate(both):
-                spec[g, :, :WIDE] = real[i * ROWS // 2 : (i + 1) * ROWS // 2]
-                spec[g, :, WIDE:] = imag[i * ROWS // 2 : (i + 1) * ROWS // 2]
-
-        pout[...] = jnp.zeros_like(pout)
-
-        @pl.loop(0, PAIRS)
+                spec[g, top : top + count, :WIDE] = real[i * count : (i + 1) * count]
+                spec[g, top : top + count, WIDE:] = imag[i * count : (i + 1) * count]
+
+        if top == 0:
+            pout[...] = jnp.zeros_like(pout)
+
+        @pl.loop(qs[0], qs[-1] + 1)
         def _(q):
             for f1 in range(8):
                 points = []
@@ -349,6 +361,9 @@
                     pout[n] += value[0] * both[:8] + value[1] * both[8:]
             pass
 
+        if qs[-1] + 1 < PAIRS:
+            return
+
         @pl.loop(0, BLOCKS // 2)
         def _(i):
             zk, row = i // 8 * 2 + i % 2, i // 2 % 4
@@ -411,12 +426,16 @@
                         out[to, at : at + 1, WIDE:] = fin[g][s, row, j, i, 1:2]
 
     for step in range(CHUNKS):
-        done(rcv.at[step], main_recv.at[step])
-        if step == 0:
-            pl.semaphore_wait(group_sem, 1)
+        if step < CHUNKS - 1:
+            done(rcv.at[step], main_recv.at[step])
         if step < 2:
             send_main(step + 1, 1)
-        convolve(step)
+        if step < CHUNKS - 1:
+            convolve(step, range(PAIRS))
+        else:
+            for q in range(PAIRS):
+                done(rcv.at[step, pl.ds(0, LONS), pl.ds(q * 16, 16)], main_recv.at[step + q])
+                convolve(step, (q,))
         if step < MIXED:
             send_sums(step)
         else:
@@ -484,7 +503,7 @@
             pltpu.VMEM((BLOCKS, 8, WIDE), F32),
             pltpu.VMEM((CHUNKS, XS) + circle, F32),
             pltpu.VMEM((CHUNKS, XS - 1) + circle, F32),
-            dma((8,)), dma, dma, dma, dma, dma((CHUNKS,)), dma((CHUNKS,)),
+            dma((8,)), dma, dma, dma, dma, dma((CHUNKS,)), dma((CHUNKS + 1,)),
             dma((CHUNKS,)), dma((CHUNKS,)), dma((CHUNKS,)), dma((CHUNKS,)), dma((CHUNKS,)), dma((CHUNKS,)),
             dma((CHUNKS,)), dma((CHUNKS,)), pltpu.SemaphoreType.REGULAR,
         ]

time: 78.5 us -> 76.7 us (0.977)
  Pallas kernels: 76.4 us -> 74.7 us
    pallas_call x1, Pallas kernels: 76.4 us -> 74.7 us  [per_device(): pl.pallas_call(kernel, out_shape=jax.ShapeDtypeStruct((LONS, LATS, 2 * WI...]
where the time goes in v4:
time: 76.7 us; the launch traced here: 76.6 us
  Pallas kernels  74.7 us (97%)
  other arithmetic  1.89 us (2%)
    pallas_call x1, Pallas kernels, per_device(): pl.pallas_call(kernel, out_shape=jax.ShapeDtypeStruct((LONS, LATS, 2 * WI...  74.7 us
    div x1, other arithmetic, per_device(): return total.reshape(LONS * LATS, 2 * WIDE) / (members - 1)  1.89 us

profile of v4, /device:TPU:1, one launch (start us, length us, event | category | flops | bytes accessed | tf_op | source)
XLA Modules:
  0.0 76.6 jit_solution(15238461677054575599)
XLA Ops:
  0.0 74.7 %localize.1 = f32[32,16,256]{2,1,0:T(8,128)} custom-call(bf16[8,512,256]{2,1,0:T(8,128)(2,1)} %a_hbm.1, bf16[512,256]{1,0:T(8,128)(2,1)} %inc_hbm.1, f32[64,128]{1,0:T(8,128)} %bitcast.2, f32[256,64]{1,0:T(8,128)} %constant.11.clone.first_hbm, f32[2,128,128]{2,1,0:T(8,128)} %constant.12.clone.twist_hbm, f32[2,64,128]{2,1,0:T(8,128)} %constant.13.clone.back_hbm, ...), custom_call_target="tpu_custom_call" | custom-call | tf_op jit(solution)/shard_map/localize/pallas_call | solution.py:481
  74.7 1.9 %broadcast_multiply_fusion = f32[32,16,256]{2,1,0:T(8,128)} fusion(f32[32,16,256]{2,1,0:T(8,128)} %localize.1), kind=kLoop, calls=%fused_computation | loop fusion | flops 131072 | bytes 1048576 | tf_op jit(solution)/shard_map/div | solution.py:520

commit v5 on v4

--- a/solution.py
+++ b/solution.py
@@ -382,35 +382,46 @@
         for d in range(1, XS):
             remote(rs_snd.at[c, xs[d]], rs_rcv.at[c, d - 1], rs_send.at[c], rs_recv.at[c], lon, mems[d])
 
+    def parts(g):
+        return ((0, 2), (2, 2)) if g == len(SETS) - 1 else ((0, 4),)
+
     def send_back(g):
         for j, c in enumerate(SETS[g]):
             if c < MIXED:
                 done(rs_rcv.at[c], rs_recv.at[c])
                 qb[g][:, j] = rs_snd[c, x] + rs_rcv[c, 0] + rs_rcv[c, 1] + rs_rcv[c, 2]
-        mine = z * 2 + k
-        for e in (1, 0):
-            for s in range(8):
-                if e or s:
-                    index = zs[s // 2] // 4 + ks[s % 2]
-                    remote(
-                        qb[g].at[index], fr[g].at[zhi, mine], ret_send.at[g], ret_recv.at[g],
-                        rows16[s], groups[e],
-                    )
-        local(qb[g].at[mine], fr[g].at[zhi, mine], ret_recv.at[g])
+        mine, all_of = z * 2 + k, pl.ds(0, len(SETS[g]))
+        for i, (row, count) in enumerate(parts(g)):
+            rows, sem = pl.ds(row, count), ret_recv.at[g + i]
+            for e in (1, 0):
+                for s in range(8):
+                    if e or s:
+                        index = zs[s // 2] // 4 + ks[s % 2]
+                        remote(
+                            qb[g].at[index, all_of, rows], fr[g].at[zhi, mine, all_of, rows],
+                            ret_send.at[g], sem, rows16[s], groups[e],
+                        )
+            local(qb[g].at[mine, all_of, rows], fr[g].at[zhi, mine, all_of, rows], sem)
 
     def send_all(g):
-        done(fr[g], ret_recv.at[g])
-        for j in range(len(SETS[g])):
-            for row in range(4):
-                part[g][row, j] = fr[g][0, :, j, row] + fr[g][1, :, j, row]
-        for d in (2, 1, 3, 0):
-            for e in (2, 1, 3, 0):
-                if d or e:
-                    there = z * 8 + ys[e] + k
-                    remote(
-                        part[g].at[ys[e] // 2], fin[g].at[x, y], fin_send.at[g], fin_recv.at[g],
-                        there, mems[d],
-                    )
+        for i, (first_row, count) in enumerate(parts(g)):
+            rows = range(first_row, first_row + count)
+            all_of = pl.ds(0, len(SETS[g]))
+            arrived = fr[g].at[pl.ds(0, 2), pl.ds(0, 8), all_of, pl.ds(first_row, count)]
+            done(arrived, ret_recv.at[g + i])
+            for row in rows:
+                for j in range(len(SETS[g])):
+                    part[g][row, j] = fr[g][0, :, j, row] + fr[g][1, :, j, row]
+
+            def send(row, d):
+                there = z * 8 + row * 2 + k
+                remote(part[g].at[row], fin[g].at[x, y], fin_send.at[g], fin_recv.at[g], there, mems[d])
+
+            for d in (2, 1, 3):
+                for row in rows:
+                    send(row, d)
+            for row in rows:
+                pl.when(y != row)(functools.partial(send, row, 0))
         local(part[g].at[y], fin[g].at[x, y], fin_recv.at[g])
 
     def assemble(g):
@@ -449,8 +460,8 @@
             send_all(1)
 
     send_all(0)
+    send_all(2)
     assemble(1)
-    send_all(2)
     assemble(0)
     assemble(2)
 

time: 76.7 us -> 76.3 us (level)
  no operation moved by 1% of the time
where the time goes in v5:
time: 76.3 us; the launch traced here: 76.2 us
  Pallas kernels  74.3 us (97%)
  other arithmetic  1.89 us (2%)
    pallas_call x1, Pallas kernels, per_device(): pl.pallas_call(kernel, out_shape=jax.ShapeDtypeStruct((LONS, LATS, 2 * WI...  74.3 us
    div x1, other arithmetic, per_device(): return total.reshape(LONS * LATS, 2 * WIDE) / (members - 1)  1.89 us

profile of v5, /device:TPU:1, one launch (start us, length us, event | category | flops | bytes accessed | tf_op | source)
XLA Modules:
  0.0 76.2 jit_solution(9147242826217564416)
XLA Ops:
  0.0 74.3 %localize.1 = f32[32,16,256]{2,1,0:T(8,128)} custom-call(bf16[8,512,256]{2,1,0:T(8,128)(2,1)} %a_hbm.1, bf16[512,256]{1,0:T(8,128)(2,1)} %inc_hbm.1, f32[64,128]{1,0:T(8,128)} %bitcast.2, f32[256,64]{1,0:T(8,128)} %constant.11.clone.first_hbm, f32[2,128,128]{2,1,0:T(8,128)} %constant.12.clone.twist_hbm, f32[2,64,128]{2,1,0:T(8,128)} %constant.13.clone.back_hbm, ...), custom_call_target="tpu_custom_call" | custom-call | tf_op jit(solution)/shard_map/localize/pallas_call | solution.py:492
  74.3 1.9 %broadcast_multiply_fusion = f32[32,16,256]{2,1,0:T(8,128)} fusion(f32[32,16,256]{2,1,0:T(8,128)} %localize.1), kind=kLoop, calls=%fused_computation | loop fusion | flops 131072 | bytes 1048576 | tf_op jit(solution)/shard_map/div | solution.py:531

commit v6 on v5

--- a/solution.py
+++ b/solution.py
@@ -383,7 +383,7 @@
             remote(rs_snd.at[c, xs[d]], rs_rcv.at[c, d - 1], rs_send.at[c], rs_recv.at[c], lon, mems[d])
 
     def parts(g):
-        return ((0, 2), (2, 2)) if g == len(SETS) - 1 else ((0, 4),)
+        return ((0, 3), (3, 1)) if g == len(SETS) - 1 else ((0, 4),)
 
     def send_back(g):
         for j, c in enumerate(SETS[g]):

time: 76.3 us -> 76.4 us (level)
  no operation moved by 1% of the time
where the time goes in v6:
time: 76.4 us; the launch traced here: 76.2 us
  Pallas kernels  74.3 us (97%)
  other arithmetic  1.89 us (2%)
    pallas_call x1, Pallas kernels, per_device(): pl.pallas_call(kernel, out_shape=jax.ShapeDtypeStruct((LONS, LATS, 2 * WI...  74.3 us
    div x1, other arithmetic, per_device(): return total.reshape(LONS * LATS, 2 * WIDE) / (members - 1)  1.89 us

profile of v6, /device:TPU:1, one launch (start us, length us, event | category | flops | bytes accessed | tf_op | source)
XLA Modules:
  0.0 76.2 jit_solution(14237743630158684742)
XLA Ops:
  0.0 74.3 %localize.1 = f32[32,16,256]{2,1,0:T(8,128)} custom-call(bf16[8,512,256]{2,1,0:T(8,128)(2,1)} %a_hbm.1, bf16[512,256]{1,0:T(8,128)(2,1)} %inc_hbm.1, f32[64,128]{1,0:T(8,128)} %bitcast.2, f32[256,64]{1,0:T(8,128)} %constant.11.clone.first_hbm, f32[2,128,128]{2,1,0:T(8,128)} %constant.12.clone.twist_hbm, f32[2,64,128]{2,1,0:T(8,128)} %constant.13.clone.back_hbm, ...), custom_call_target="tpu_custom_call" | custom-call | tf_op jit(solution)/shard_map/localize/pallas_call | solution.py:492
  74.3 1.9 %broadcast_multiply_fusion = f32[32,16,256]{2,1,0:T(8,128)} fusion(f32[32,16,256]{2,1,0:T(8,128)} %localize.1), kind=kLoop, calls=%fused_computation | loop fusion | flops 131072 | bytes 1048576 | tf_op jit(solution)/shard_map/div | solution.py:531
